TPU v7x, 32 devices: a whole 2x2x4 slice. The times are simulated.
32 devices in a mesh: term: 4 (over z), sector: 8 (over y, x, core).
Axes of the slice: x: 2, y: 2, z: 4, core: 2. Of those that a mesh axis runs over, the one named last changes fastest.
Arguments:
- left_ops: float32 [4, 8, 512, 512], P('term', 'sector'), may hold values from -1 to 2, as said below
- right_ops: float32 [4, 8, 512, 512], P('term', 'sector'), may hold values from -1 to 2, as said below
- hop_left: float32 [4, 8, 512, 512], P('term', 'sector'), may hold values from -0.09375 to 0.09375
- hop_right: float32 [4, 8, 512, 512], P('term', 'sector'), may hold values from -0.09375 to 0.09375
- v_left: bfloat16 [4, 8, 512, 128], P('term', 'sector'), may hold values from -0.5 to 0.5
- v_right: bfloat16 [4, 8, 128, 512], P('term', 'sector'), may hold values from -1.5 to 1.5
- zero_blocks: bfloat16 [8, 128, 128], P('sector'), may hold values from -6 to 6
- links: int32 [4, 8], P('term', 'sector'), may hold values from 0 to 7
- block_dims: int32 [8], P('sector'), may hold values from 128 to 512
Outputs:
- solution: float32 [8, 512, 512], P('sector')
- residual: float32 [8, 512, 512], P('sector')
Inputs may be any that keep to these rules, and one draw needn't show every extreme that they name: Every block left_ops[t, s] and right_ops[t, s] is symmetric and positive definite. `right_ops`: every block is symmetric and positive definite.
All inputs are finite; a program needn't handle non-finite values.
Results may differ from a plain program's by a relative error of at most 0.0003.
Values may be sent and summed in bfloat16 or wider, within the bound.
A program may use at most 64 MiB of HBM per device.

v0:
```python
import jax
import jax.numpy as jnp
from jax import lax
from jax.sharding import PartitionSpec as P

ITERS = 3


level_gap = 2.5
exact = lax.Precision.HIGHEST


def shifted(value, axis, steps):
    count = lax.axis_size(axis)
    first, last = (max(0, -steps), min(count, count - steps))
    return lax.ppermute(value, axis, [(source, source + steps) for source in range(first, last)])


def apply_terms(field, left_op, right_op, hop_in, hop_out):
    behind = jnp.einsum("tji,jk->tik", hop_in, field, precision=exact)
    handed = jnp.einsum("tik,tlk->il", behind, hop_out, precision=exact)
    arrived = shifted(handed, "sector", 1)
    after = shifted(field, "sector", -1)
    inner_part = jnp.einsum("tij,jk->tik", left_op, field, precision=exact)
    running = jnp.einsum("tik,tkl->il", inner_part, right_op, precision=exact)
    ahead = jnp.einsum("tij,jk->tik", hop_in, after, precision=exact)
    running = running + jnp.einsum("tik,tkl->il", ahead, hop_out, precision=exact)
    return running + arrived


def body(left_ops, right_ops, hop_left, hop_right, v_left, v_right, zero_blocks, links, block_dims):
    width = left_ops.shape[-1]
    share = width // lax.axis_size("term")
    offset = lax.axis_index("term") * share
    positions = lax.iota(jnp.int32, width)
    live = positions < block_dims[0]
    live_mask = jnp.logical_and(live[:, None], live[None, :]).astype(jnp.float32)
    left_op = left_ops[:, 0]
    right_op = right_ops[:, 0]
    hop_in = hop_left[:, 0]
    hop_out = hop_right[:, 0]
    everyone = lax.all_gather(zero_blocks, "sector", axis=0, tiled=True)
    picked = everyone[links[:, 0]]
    middle = jnp.einsum("tij,tjk->tik", v_left[:, 0], picked, preferred_element_type=jnp.float32)
    source_part = jnp.einsum(
        "tik,tkl->il", middle, v_right[:, 0].astype(jnp.float32), precision=exact
    )
    local_mask = lax.dynamic_slice_in_dim(live_mask, offset, share, 0)
    source = -local_mask * lax.psum_scatter(source_part, "term", scatter_dimension=0, tiled=True)

    def operate(vector):
        whole_rows = lax.all_gather(vector, "term", axis=0, tiled=True)
        summed = lax.psum_scatter(
            apply_terms(whole_rows, left_op, right_op, hop_in, hop_out),
            "term",
            scatter_dimension=0,
            tiled=True,
        )
        return local_mask * (level_gap * vector + summed)

    def own_rows(product):
        return jnp.sum(product)

    def paired(vector, image_vec):
        return lax.psum(
            (own_rows(vector * vector), own_rows(vector * image_vec)), ("term", "sector")
        )

    solution = jnp.zeros_like(source)
    residual = source
    image_vec = operate(residual)
    norm_now, product = paired(residual, image_vec)
    step_size = norm_now / product
    direction = residual
    along = image_vec
    for sweep_index in range(ITERS):
        solution = solution + step_size * direction
        residual = residual - step_size * along
        if sweep_index + 1 < ITERS:
            image_vec = operate(residual)
            norm_next, product = paired(residual, image_vec)
            ratio = norm_next / norm_now
            step_size = norm_next / (product - ratio * norm_next / step_size)
            direction = residual + ratio * direction
            along = image_vec + ratio * along
            norm_now = norm_next
    solution, residual = (
        lax.all_gather(solution, "term", axis=0, tiled=True),
        lax.all_gather(residual, "term", axis=0, tiled=True),
    )
    return (solution[None], residual[None])


def solution(mesh):
    return jax.shard_map(
        body,
        mesh=mesh,
        in_specs=(
            P("term", "sector", None, None),
            P("term", "sector", None, None),
            P("term", "sector", None, None),
            P("term", "sector", None, None),
            P("term", "sector", None, None),
            P("term", "sector", None, None),
            P("sector", None, None),
            P("term", "sector"),
            P("sector"),
        ),
        out_specs=(P("sector", None, None), P("sector", None, None)),
        check_vma=False,
    )
```

profile of v0, /device:TPU:0, one launch (start us, length us, event | category | flops | bytes accessed | tf_op | source)
XLA Modules:
  0.0 517.7 jit_solution(16638892782941754885)
XLA Ops:
  8.0 11.1 %all_gather.18 = bf16[8,128,128]{2,1,0:T(8,128)(2,1)S(1)} all-gather(bf16[1,128,128]{2,1,0:T(8,128)(2,1)} %param.15), channel_id=1, replica_groups=mesh['term'=4,'sector'=8] {'sector'}, dimensions={0}, use_global_device_ids=true | all-gather | bytes 294912 | tf_op jit(solution)/shard_map/all_gather | solution.py:42
  20.0 1.6 fusion.37
  22.4 26.8 %reduce-scatter.5.cloned.1.call-done = f32[128,512]{1,0:T(8,128)} async-done(((f32[512,512]{1,0:T(8,128)}), f32[128,512]{1,0:T(8,128)}) %reduce-scatter.5.cloned.1.call-update) | async-done | bytes 262160 | tf_op jit(solution)/shard_map/reduce_scatter | solution.py:49
  49.2 1.8 fusion.36
  51.1 27.0 %all-gather.6.cloned.1.call-done = f32[512,512]{1,0:T(8,128)} async-done(((f32[128,512]{1,0:T(8,128)}), f32[512,512]{1,0:T(8,128)}) %all-gather.6.cloned.1.call-update) | async-done | bytes 1048592 | tf_op jit(solution)/shard_map/all_gather | solution.py:52
  78.1 1.3 collective-permute-start
  79.4 3.1 fusion.20
  82.5 3.5 fusion.9
  86.0 3.5 collective-permute-start.1
  89.5 3.5 fusion.34
  93.0 1.9 fusion.28
  94.9 3.6 fusion.22
  98.5 3.0 fusion.2
  101.5 34.0 %reduce-scatter.7.cloned.1.call-done = f32[128,512]{1,0:T(8,128)} async-done(((f32[512,512]{1,0:T(8,128)}), f32[128,512]{1,0:T(8,128)}) %reduce-scatter.7.cloned.1.call-update) | async-done | bytes 262160 | tf_op jit(solution)/shard_map/reduce_scatter | solution.py:53
  135.6 1.7 multiply_reduce_fusion.4
  137.3 39.1 %all-reduce.2 = (f32[]{:T(128)}, f32[]{:T(128)}) all-reduce(f32[]{:T(128)} %get-tuple-element.18, f32[]{:T(128)} %get-tuple-element.17), channel_id=1, replica_groups=mesh['term'=4,'sector'=8] {'term','sector'}, use_global_device_ids=true, to_apply=%region_2.0 | all-reduce | flops 2 | bytes 16 | tf_op jit(solution)/shard_map/psum | solution.py:65
  177.7 1.8 multiply_subtract_fusion.2
  179.5 12.1 %reduce-scatter.9.cloned.1.call-start = ((), (), s32[]{:S(2)}) async-start(), calls=%async_computation.8 | async-start | bytes 1310720 | tf_op jit(solution)/shard_map/reduce_scatter | solution.py:53
  191.6 16.0 %all-gather.8.cloned.1.call-done = f32[512,512]{1,0:T(8,128)} async-done(((f32[128,512]{1,0:T(8,128)}), f32[512,512]{1,0:T(8,128)}) %all-gather.8.cloned.1.call-update) | async-done | bytes 1048592 | tf_op jit(solution)/shard_map/all_gather | solution.py:52
  207.6 3.2 fusion.16
  210.8 1.3 collective-permute-start.2
  212.1 3.5 fusion.6
  215.6 3.2 collective-permute-start.3
  218.8 3.5 fusion.32
  222.3 1.8 fusion.26
  224.2 3.5 fusion.18
  227.7 2.8 fusion.1
  230.6 37.4 %reduce-scatter.9.cloned.1.call-done = f32[128,512]{1,0:T(8,128)} async-done(((f32[512,512]{1,0:T(8,128)}), f32[128,512]{1,0:T(8,128)}) %reduce-scatter.9.cloned.1.call-update) | async-done | bytes 262160 | tf_op jit(solution)/shard_map/reduce_scatter | solution.py:53
  268.0 1.8 multiply_reduce_fusion.2
  269.8 39.1 %all-reduce.1 = (f32[]{:T(128)}, f32[]{:T(128)}) all-reduce(f32[]{:T(128)} %get-tuple-element.16, f32[]{:T(128)} %get-tuple-element.15), channel_id=1, replica_groups=mesh['term'=4,'sector'=8] {'term','sector'}, use_global_device_ids=true, to_apply=%region_7.0 | all-reduce | flops 2 | bytes 16 | tf_op jit(solution)/shard_map/psum | solution.py:65
  313.2 2.1 multiply_subtract_fusion.1
  315.6 27.8 %all-gather.10.cloned.1.call-done = f32[512,512]{1,0:T(8,128)} async-done(((f32[128,512]{1,0:T(8,128)}), f32[512,512]{1,0:T(8,128)}) %all-gather.10.cloned.1.call-update) | async-done | bytes 1048592 | tf_op jit(solution)/shard_map/all_gather | solution.py:52
  343.4 3.2 fusion.12
  346.6 1.3 collective-permute-start.4
  347.9 3.5 fusion.3
  351.4 3.2 collective-permute-start.5
  354.6 3.5 fusion.30
  358.1 1.8 fusion.24
  360.0 3.5 fusion.14
  363.5 2.8 fusion
  366.4 37.4 %reduce-scatter.11.cloned.1.call-done = f32[128,512]{1,0:T(8,128)} async-done(((f32[512,512]{1,0:T(8,128)}), f32[128,512]{1,0:T(8,128)}) %reduce-scatter.11.cloned.1.call-update) | async-done | bytes 262160 | tf_op jit(solution)/shard_map/reduce_scatter | solution.py:53
  403.8 1.8 multiply_reduce_fusion
  405.5 39.1 %all-reduce = (f32[]{:T(128)}, f32[]{:T(128)}) all-reduce(f32[]{:T(128)} %get-tuple-element.14, f32[]{:T(128)} %get-tuple-element.13), channel_id=1, replica_groups=mesh['term'=4,'sector'=8] {'term','sector'}, use_global_device_ids=true, to_apply=%region_12.0 | all-reduce | flops 2 | bytes 16 | tf_op jit(solution)/shard_map/psum | solution.py:65
  448.7 1.0 multiply_subtract_fusion
  450.4 27.4 %all-gather.12.cloned.1.call-done = f32[512,512]{1,0:T(8,128)} async-done(((f32[128,512]{1,0:T(8,128)}), f32[512,512]{1,0:T(8,128)}) %all-gather.12.cloned.1.call-update) | async-done | bytes 1048592 | tf_op jit(solution)/shard_map/all_gather | solution.py:88
  477.8 29.6 %all-gather.14.cloned.1.call-done = f32[512,512]{1,0:T(8,128)} async-done(((f32[128,512]{1,0:T(8,128)}), f32[512,512]{1,0:T(8,128)}) %all-gather.14.cloned.1.call-update) | async-done | bytes 1048592 | tf_op jit(solution)/shard_map/all_gather | solution.py:89
  507.4 2.4 copy.15
  509.8 1.0 copy.16
  (60 shorter events, 2.4 us)
Async XLA Ops:
  7.2 72.2 %copy-start = (f32[1,1,512,512]{3,2,1,0:T(8,128)S(1)}, f32[1,1,512,512]{3,2,1,0:T(8,128)}, u32[]{:S(2)}) copy-start(f32[1,1,512,512]{3,2,1,0:T(8,128)} %param.11) | copy-start | bytes 3145732
  7.2 42.0 %reduce-scatter.5.cloned.1.call-start = ((), (), s32[]{:S(2)}) async-start(), calls=%async_computation.4 | async-start | bytes 1310720 | tf_op jit(solution)/shard_map/reduce_scatter | solution.py:49
  8.0 11.1 %copy-start.15 = (bf16[1,1,512,128]{3,2,1,0:T(8,128)(2,1)S(1)}, bf16[1,1,512,128]{3,2,1,0:T(8,128)(2,1)}, u32[]{:S(2)}) copy-start(bf16[1,1,512,128]{3,2,1,0:T(8,128)(2,1)} %param.13) | copy-start | bytes 393220
  19.1 0.9 copy-start.16
  21.6 56.5 %all-gather.6.cloned.1.call-start = ((), (), s32[]{:S(2)}) async-start(), calls=%async_computation.5 | async-start | bytes 1310720 | tf_op jit(solution)/shard_map/all_gather | solution.py:52
  51.0 31.5 %copy-start.1 = (f32[1,1,512,512]{3,2,1,0:T(8,128)S(1)}, f32[1,1,512,512]{3,2,1,0:T(8,128)}, u32[]{:S(2)}) copy-start(f32[1,1,512,512]{3,2,1,0:T(8,128)} %param.12) | copy-start | bytes 3145732
  51.0 84.5 %reduce-scatter.7.cloned.1.call-start = ((), (), s32[]{:S(2)}) async-start(), calls=%async_computation.6 | async-start | bytes 1310720 | tf_op jit(solution)/shard_map/reduce_scatter | solution.py:53
  78.1 16.8 %collective-permute-start = (f32[512,512]{1,0:T(8,128)}, f32[512,512]{1,0:T(8,128)S(1)}, u32[]{:S(2)}, u32[]{:S(2)}) collective-permute-start(f32[512,512]{1,0:T(8,128)} %all-gather.6.cloned.1.call-done), channel_id=1, source_target_pairs={{1,0},{2,1},{3,2},{4,3},{5,4},{6,5},{7,6},{9,8},{10,9},{11,10},{12... | collective-permute-start | bytes 3145736 | tf_op jit(solution)/shard_map/ppermute | solution.py:16
  82.5 7.0 %copy-start.2 = (f32[1,1,512,512]{3,2,1,0:T(8,128)S(1)}, f32[1,1,512,512]{3,2,1,0:T(8,128)}, u32[]{:S(2)}) copy-start(f32[1,1,512,512]{3,2,1,0:T(8,128)} %param.9) | copy-start | bytes 3145732
  82.5 7.0 %copy-start.8 = (f32[512,512]{1,0:T(8,128)S(1)}, f32[512,512]{1,0:T(8,128)}, u32[]{:S(2)}) copy-start(f32[512,512]{1,0:T(8,128)} %all-gather.6.cloned.1.call-done) | copy-start | bytes 3145732
  86.0 7.0 %copy-start.3 = (f32[1,1,512,512]{3,2,1,0:T(8,128)S(1)}, f32[1,1,512,512]{3,2,1,0:T(8,128)}, u32[]{:S(2)}) copy-start(f32[1,1,512,512]{3,2,1,0:T(8,128)} %param.10) | copy-start | bytes 3145732
  86.0 12.5 %collective-permute-start.1 = (f32[512,512]{1,0:T(8,128)S(1)}, f32[512,512]{1,0:T(8,128)S(1)}, u32[]{:S(2)}, u32[]{:S(2)}) collective-permute-start(f32[512,512]{1,0:T(8,128)S(1)} %fusion.9), channel_id=1, source_target_pairs={{0,1},{1,2},{2,3},{3,4},{4,5},{5,6},{6,7},{8,9},{9,10},{10,11},{11... | collective-permute-start | bytes 3145736 | tf_op jit(solution)/shard_map/ppermute | solution.py:16
  101.5 34.1 %copy-start.6 = (f32[128,512]{1,0:T(8,128)S(1)}, f32[128,512]{1,0:T(8,128)}, u32[]{:S(2)}) copy-start(f32[128,512]{1,0:T(8,128)} %reduce-scatter.5.cloned.1.call-done) | copy-start | bytes 786436
  101.5 106.1 %all-gather.8.cloned.1.call-start = ((), (), s32[]{:S(2)}) async-start(), calls=%async_computation.7 | async-start | bytes 1310720 | tf_op jit(solution)/shard_map/all_gather | solution.py:52
  179.5 88.4 %reduce-scatter.9.cloned.1.call-start = ((), (), s32[]{:S(2)}) async-start(), calls=%async_computation.8 | async-start | bytes 1310720 | tf_op jit(solution)/shard_map/reduce_scatter | solution.py:53
  207.6 3.2 copy-start.9
  210.8 13.4 %collective-permute-start.2 = (f32[512,512]{1,0:T(8,128)S(1)}, f32[512,512]{1,0:T(8,128)S(1)}, u32[]{:S(2)}, u32[]{:S(2)}) collective-permute-start(f32[512,512]{1,0:T(8,128)S(1)} %copy-done.9), channel_id=1, source_target_pairs={{1,0},{2,1},{3,2},{4,3},{5,4},{6,5},{7,6},{9,8},{10,9},{11,10},{12... | collective-permute-start | bytes 3145736 | tf_op jit(solution)/shard_map/ppermute | solution.py:16
  215.6 6.7 %copy-start.4 = (f32[1,1,512,512]{3,2,1,0:T(8,128)S(1)}, f32[1,1,512,512]{3,2,1,0:T(8,128)}, u32[]{:S(2)}) copy-start(f32[1,1,512,512]{3,2,1,0:T(8,128)} %param.10) | copy-start | bytes 3145732
  215.6 12.1 %collective-permute-start.3 = (f32[512,512]{1,0:T(8,128)S(1)}, f32[512,512]{1,0:T(8,128)S(1)}, u32[]{:S(2)}, u32[]{:S(2)}) collective-permute-start(f32[512,512]{1,0:T(8,128)S(1)} %fusion.6), channel_id=1, source_target_pairs={{0,1},{1,2},{2,3},{3,4},{4,5},{5,6},{6,7},{8,9},{9,10},{10,11},{11... | collective-permute-start | bytes 3145736 | tf_op jit(solution)/shard_map/ppermute | solution.py:16
  230.5 112.9 %all-gather.10.cloned.1.call-start = ((), (), s32[]{:S(2)}) async-start(), calls=%async_computation.9 | async-start | bytes 1310720 | tf_op jit(solution)/shard_map/all_gather | solution.py:52
  315.3 88.4 %reduce-scatter.11.cloned.1.call-start = ((), (), s32[]{:S(2)}) async-start(), calls=%async_computation.10 | async-start | bytes 1310720 | tf_op jit(solution)/shard_map/reduce_scatter | solution.py:53
  343.4 3.2 copy-start.10
  346.6 13.4 %collective-permute-start.4 = (f32[512,512]{1,0:T(8,128)S(1)}, f32[512,512]{1,0:T(8,128)S(1)}, u32[]{:S(2)}, u32[]{:S(2)}) collective-permute-start(f32[512,512]{1,0:T(8,128)S(1)} %copy-done.10), channel_id=1, source_target_pairs={{1,0},{2,1},{3,2},{4,3},{5,4},{6,5},{7,6},{9,8},{10,9},{11,10},{12... | collective-permute-start | bytes 3145736 | tf_op jit(solution)/shard_map/ppermute | solution.py:16
  351.4 6.7 %copy-start.5 = (f32[1,1,512,512]{3,2,1,0:T(8,128)S(1)}, f32[1,1,512,512]{3,2,1,0:T(8,128)}, u32[]{:S(2)}) copy-start(f32[1,1,512,512]{3,2,1,0:T(8,128)} %param.10) | copy-start | bytes 3145732
  351.4 12.1 %collective-permute-start.5 = (f32[512,512]{1,0:T(8,128)S(1)}, f32[512,512]{1,0:T(8,128)S(1)}, u32[]{:S(2)}, u32[]{:S(2)}) collective-permute-start(f32[512,512]{1,0:T(8,128)S(1)} %fusion.3), channel_id=1, source_target_pairs={{0,1},{1,2},{2,3},{3,4},{4,5},{5,6},{6,7},{8,9},{9,10},{10,11},{11... | collective-permute-start | bytes 3145736 | tf_op jit(solution)/shard_map/ppermute | solution.py:16
  366.3 37.5 %copy-start.11 = (f32[128,512]{1,0:T(8,128)S(1)}, f32[128,512]{1,0:T(8,128)}, u32[]{:S(2)}) copy-start(f32[128,512]{1,0:T(8,128)} %get-tuple-element.25) | copy-start | bytes 786436
  366.3 82.3 %copy-start.14 = (f32[128,512]{1,0:T(8,128)S(1)}, f32[128,512]{1,0:T(8,128)}, u32[]{:S(2)}) copy-start(f32[128,512]{1,0:T(8,128)} %get-tuple-element.26) | copy-start | bytes 786436
  366.3 82.3 %copy-start.7 = (f32[128,512]{1,0:T(8,128)S(1)}, f32[128,512]{1,0:T(8,128)}, u32[]{:S(2)}) copy-start(f32[128,512]{1,0:T(8,128)} %multiply_subtract_fusion.2) | copy-start | bytes 786436
  366.3 111.5 %all-gather.12.cloned.1.call-start = ((), (), s32[]{:S(2)}) async-start(), calls=%async_computation.11 | async-start | bytes 1310720 | tf_op jit(solution)/shard_map/all_gather | solution.py:88
  403.8 44.9 %copy-start.13 = (f32[128,512]{1,0:T(8,128)S(1)}, f32[128,512]{1,0:T(8,128)}, u32[]{:S(2)}) copy-start(f32[128,512]{1,0:T(8,128)} %reduce-scatter.11.cloned.1.call-done) | copy-start | bytes 786436
  449.7 57.7 %all-gather.14.cloned.1.call-start = ((), (), s32[]{:S(2)}) async-start(), calls=%async_computation.12 | async-start | bytes 1310720 | tf_op jit(solution)/shard_map/all_gather | solution.py:89
  507.4 2.4 copy-start.12
Sparse Core Ops, SparseCore 0:
  21.7 27.4 reduce-scatter.4
  51.4 26.5 all-gather.5
  101.6 33.9 reduce-scatter.6
  179.6 27.9 all-gather.7
  230.7 37.2 reduce-scatter.8
  315.5 27.9 all-gather.9
  366.5 37.2 reduce-scatter.10
  449.8 27.9 all-gather.11
  480.0 27.4 all-gather.13
where the time goes:
time: 524 us; the launch traced here: 518 us
  waiting for transfers between devices  264 us (50%)
  blocking collectives  128 us (24%)
  matrix products  56.8 us (11%)
  starting transfers between devices  26.4 us (5%)
  between operations  25.7 us (5%)
  other arithmetic  12 us (2%)
    psum x3, blocking collectives, paired(): lax.psum((own_rows(vector * vector), own_rows(vector * image_vec)), ('ter...  117 us
    reduce_scatter x3, waiting for transfers between devices, operate(): lax.psum_scatter(apply_terms(whole_rows, left_op, right_op, hop_in, hop_o...  109 us
    all_gather x3, waiting for transfers between devices, operate(): whole_rows = lax.all_gather(vector, 'term', axis=0, tiled=True)  70.9 us
    all_gather x1, waiting for transfers between devices, body(): lax.all_gather(residual, 'term', axis=0, tiled=True)  29.6 us
    all_gather x1, waiting for transfers between devices, body(): lax.all_gather(solution, 'term', axis=0, tiled=True)  27.4 us
    reduce_scatter x1, waiting for transfers between devices, body(): lax.psum_scatter(source_part, 'term', scatter_dimension=0, tiled=True)  26.8 us
    ppermute x6, starting transfers between devices, shifted(): lax.ppermute(value, axis, [(source, source + steps) for source in range(f...  13.8 us
    reduce_scatter x3, starting transfers between devices, operate(): lax.psum_scatter(apply_terms(whole_rows, left_op, right_op, hop_in, hop_o...  12.4 us
  transfers between devices with their start and end apart: 15, of which 9 were waited for; matrix products, arithmetic and copies ran while one was open for 8% of the time, Pallas kernels for 0%

commit v1 on v0

v1 whole, which is shorter than its diff:
```python
import functools

import jax
import jax.numpy as jnp
from jax import lax
from jax.experimental import pallas as pl
from jax.experimental.pallas import tpu as pltpu
from jax.sharding import PartitionSpec as P

ITERS = 3
CHUNKS = 8
GROUPS = 4

level_gap = 2.5
MESH = pl.DeviceIdType.MESH
f32 = jnp.float32
bf16 = jnp.bfloat16


def halves(value):
    high = value.astype(bf16)
    return high, (value - high.astype(f32)).astype(bf16)


def dot(a, b):
    return jnp.dot(a, b, preferred_element_type=f32)


def dot3(a_high, a_low, b_high, b_low):
    return dot(a_high, b_high) + (dot(a_high, b_low) + dot(a_low, b_high))


def kernel(
    nz, ns, links_ref, dims_ref, left_ref, right_ref, hop_in_ref, hop_out_ref,
    v_left_ref, v_right_ref, zero_ref,
    solution_ref, residual_ref,
    zeros_all, behind_in, behind_out, stage_in, stage_out,
    field_high, field_low, fields, alongs, direction,
    images, part, from_out, from_in, marks_out, marks_in,
    zero_send, zero_recv, hop_send, hop_recv, in_send, in_recv, in_recv2, out_send,
    side_send, side_recv, mark_send, mark_recv,
):
    z = lax.axis_index("term")
    s = lax.axis_index("sector")
    width = fields.shape[-1]
    chunk = width // CHUNKS
    group = width // GROUPS
    per_group = CHUNKS // GROUPS
    mid = nz // 2
    low_half = z < mid
    inward = jnp.where(low_half, z + 1, z - 1)
    outward = jnp.where(low_half, jnp.maximum(z - 1, 0), jnp.minimum(z + 1, nz - 1))
    dist = jnp.where(low_half, mid - 1 - z, z - mid)
    is_mid = dist == 0
    has_out = dist < mid - 1
    has_prev = s > 0
    has_next = s < ns - 1
    before = jnp.maximum(s - 1, 0)
    after = jnp.minimum(s + 1, ns - 1)

    def chunk_rows(c):
        return pl.ds(pl.multiple_of(c * chunk, chunk), chunk)

    def group_rows(g):
        return pl.ds(pl.multiple_of(g * group, group), group)

    barrier = pltpu.get_barrier_semaphore()
    for step in range(1, ns):
        pl.semaphore_signal(
            barrier, inc=1, device_id=(z, lax.rem(s + step, ns)), device_id_type=MESH
        )
    pl.semaphore_signal(barrier, inc=1, device_id=(inward, s), device_id_type=MESH)

    @pl.when(has_out)
    def _():
        pl.semaphore_signal(barrier, inc=1, device_id=(outward, s), device_id_type=MESH)

    pl.semaphore_wait(barrier, ns + jnp.where(has_out, 1, 0))

    def zero_copy(step):
        return pltpu.make_async_remote_copy(
            src_ref=zero_ref,
            dst_ref=zeros_all.at[s],
            send_sem=zero_send.at[step],
            recv_sem=zero_recv.at[step],
            device_id=(z, lax.rem(s + step, ns)),
            device_id_type=MESH,
        )

    for step in range(1, ns):
        zero_copy(step).start()
    zeros_all[s] = zero_ref[...]

    hop_copies = [
        pltpu.make_async_remote_copy(
            src_ref=src,
            dst_ref=dst,
            send_sem=hop_send.at[i],
            recv_sem=hop_recv.at[i],
            device_id=(z, after),
            device_id_type=MESH,
        )
        for i, (src, dst) in enumerate(((hop_in_ref, behind_in), (hop_out_ref, behind_out)))
    ]

    @pl.when(has_next)
    def _():
        for copy in hop_copies:
            copy.start()

    @pl.when(jnp.logical_not(has_prev))
    def _():
        behind_in[...] = jnp.zeros_like(behind_in)
        behind_out[...] = jnp.zeros_like(behind_out)
        for parity in range(2):
            images[parity, 2] = jnp.zeros((width, width), f32)

    @pl.when(jnp.logical_not(has_next))
    def _():
        for parity in range(2):
            images[parity, 1] = jnp.zeros((width, width), f32)

    live_count = dims_ref[0]

    def mask_rows(start, rows):
        row = lax.broadcasted_iota(jnp.int32, (rows, width), 0) + start
        column = lax.broadcasted_iota(jnp.int32, (rows, width), 1)
        live = jnp.logical_and(row < live_count, column < live_count)
        return jnp.where(live, 1.0, 0.0).astype(f32)

    def to_middle(parity, c):
        return pltpu.make_async_remote_copy(
            src_ref=part.at[parity, chunk_rows(c)],
            dst_ref=from_in.at[parity, chunk_rows(c)],
            send_sem=in_send.at[parity, c],
            recv_sem=in_recv.at[parity, c],
            device_id=(inward, s),
            device_id_type=MESH,
        )

    def to_inward(parity, c):
        return pltpu.make_async_remote_copy(
            src_ref=part.at[parity, chunk_rows(c)],
            dst_ref=from_out.at[parity, chunk_rows(c)],
            send_sem=in_send.at[parity, c],
            recv_sem=in_recv2.at[parity, c],
            device_id=(inward, s),
            device_id_type=MESH,
        )

    def to_outward(parity, c):
        return pltpu.make_async_remote_copy(
            src_ref=from_in.at[parity, chunk_rows(c)],
            dst_ref=from_in.at[parity, chunk_rows(c)],
            send_sem=out_send.at[parity, c],
            recv_sem=in_recv.at[parity, c],
            device_id=(outward, s),
            device_id_type=MESH,
        )

    def to_side(parity, c, which):
        return pltpu.make_async_remote_copy(
            src_ref=images.at[parity, 0, chunk_rows(c)],
            dst_ref=images.at[parity, which, chunk_rows(c)],
            send_sem=side_send.at[parity, which - 1, c],
            recv_sem=side_recv.at[parity, which - 1, c],
            device_id=(z, before if which == 1 else after),
            device_id_type=MESH,
        )

    def reduce_rows(parity, produce, finish, share):
        most = 2 + 2 * (mid - 1)
        lag = 2 + 2 * dist

        def one(c, carry):
            @pl.when(c < CHUNKS)
            def _():
                @pl.when(lax.rem(c, per_group) == 0)
                def _():
                    produce(c // per_group)

                @pl.when(has_out)
                def _():
                    to_inward(parity, c).wait_recv()
                    part[parity, chunk_rows(c)] = (
                        part[parity, chunk_rows(c)] + from_out[parity, chunk_rows(c)]
                    )

                @pl.when(is_mid)
                def _():
                    to_middle(parity, c).start()

                @pl.when(jnp.logical_not(is_mid))
                def _():
                    to_inward(parity, c).start()

            @pl.when(jnp.logical_and(c >= lag, c < CHUNKS + lag))
            def _():
                d = c - lag
                to_middle(parity, d).wait_recv()

                @pl.when(is_mid)
                def _():
                    from_in[parity, chunk_rows(d)] = (
                        part[parity, chunk_rows(d)] + from_in[parity, chunk_rows(d)]
                    )

                @pl.when(has_out)
                def _():
                    to_outward(parity, d).start()

                images[parity, 0, chunk_rows(d)] = finish(from_in[parity, chunk_rows(d)], d)

                if share:
                    @pl.when(has_prev)
                    def _():
                        to_side(parity, d, 1).start()

                    @pl.when(has_next)
                    def _():
                        to_side(parity, d, 2).start()

            return carry

        lax.fori_loop(0, CHUNKS + most, one, 0)

    def settle(parity, share):
        def one(c, carry):
            to_middle(parity, c).wait_send()

            @pl.when(has_out)
            def _():
                to_outward(parity, c).wait_send()

            if share:
                @pl.when(has_prev)
                def _():
                    to_side(parity, c, 1).wait_send()
                    to_side(parity, c, 2).wait_recv()

                @pl.when(has_next)
                def _():
                    to_side(parity, c, 2).wait_send()
                    to_side(parity, c, 1).wait_recv()

            return carry

        lax.fori_loop(0, CHUNKS, one, 0)

    for step in range(1, ns):
        zero_copy(step).wait()
    picked = zeros_all[links_ref[0, 0]]

    def source_rows(g):
        rows = group_rows(g)
        middle = dot(v_left_ref[rows, :], picked)
        high, rest = halves(middle)
        low = (middle - high.astype(f32)) - rest.astype(f32)
        v_right = v_right_ref[...]
        part[0, rows] = dot(high, v_right) + (
            dot(rest, v_right) + dot(low.astype(bf16), v_right)
        )

    def source_end(total, c):
        return -mask_rows(c * chunk, chunk) * total

    def split_into(slot, target, value, rows):
        high, low = halves(value)
        target[slot, 0, rows] = high
        target[slot, 1, rows] = low

    for g in range(GROUPS):
        rows = slice(g * group, (g + 1) * group)
        split_into(0, stage_in, left_ref[rows, :], rows)
        split_into(1, stage_in, hop_in_ref[rows, :], rows)
        split_into(0, stage_out, right_ref[rows, :], rows)
        split_into(1, stage_out, hop_out_ref[rows, :], rows)

    reduce_rows(0, source_rows, source_end, True)

    @pl.when(has_prev)
    def _():
        for copy in hop_copies:
            copy.wait_recv()

    for g in range(GROUPS):
        rows = slice(g * group, (g + 1) * group)
        split_into(2, stage_in, behind_in[:, rows].T, rows)
        split_into(2, stage_out, behind_out[:, rows].T, rows)

    settle(0, True)

    def fold(value):
        rows = value.shape[0]
        total = jnp.sum(value.reshape(rows // 8, 8, width), axis=0)
        return sum(total[:, i:i + 128] for i in range(0, width, 128))

    def begin(c, carry):
        rows = chunk_rows(c)
        marks = jnp.zeros((8, 128), f32)
        for which in range(3):
            value = images[0, which, rows]
            fields[which, rows] = value
            alongs[which, rows] = jnp.zeros_like(value)
            high, low = halves(value)
            field_high[which, rows] = high
            field_low[which, rows] = low
            if which == 0:
                marks = fold(value * value)
        direction[rows] = jnp.zeros((chunk, width), f32)
        solution_ref[rows, :] = jnp.zeros((chunk, width), f32)
        return carry + marks

    norm_marks = lax.fori_loop(0, CHUNKS, begin, jnp.zeros((8, 128), f32))

    def operator_rows(parity):
        def rows_of(g):
            rows = group_rows(g)
            total = None
            for which in range(3):
                first = dot3(
                    stage_in[which, 0, rows], stage_in[which, 1, rows],
                    field_high[which], field_low[which],
                )
                high, low = halves(first)
                second = dot3(high, low, stage_out[which, 0], stage_out[which, 1])
                total = second if total is None else total + second
            part[parity, rows] = total
        return rows_of

    norm_before = jnp.ones((1, 1), f32)
    step_size = jnp.ones((1, 1), f32)
    for sweep in range(ITERS):
        last = sweep + 1 == ITERS
        parity = (sweep + 1) % 2

        marks_out[sweep, 0:8] = norm_marks
        marks_out[sweep, 8:16] = jnp.zeros((8, 128), f32)

        def image_end(total, c):
            rows = chunk_rows(c)
            own = fields[0, rows]
            image = mask_rows(c * chunk, chunk) * (level_gap * own + total)
            marks_out[sweep, 8:16] = marks_out[sweep, 8:16] + fold(own * image)
            return image

        reduce_rows(parity, operator_rows(parity), image_end, not last)

        def mark_copy(step):
            return pltpu.make_async_remote_copy(
                src_ref=marks_out.at[sweep],
                dst_ref=marks_in.at[sweep, s],
                send_sem=mark_send.at[sweep, step],
                recv_sem=mark_recv.at[sweep, step],
                device_id=(z, lax.rem(s + step, ns)),
                device_id_type=MESH,
            )

        for step in range(1, ns):
            mark_copy(step).start()
        marks_in[sweep, s] = marks_out[sweep]
        settle(parity, not last)
        for step in range(1, ns):
            mark_copy(step).wait()
        summed = jnp.sum(marks_in[sweep], axis=0)
        norm_now = jnp.sum(summed[0:8], keepdims=True)
        product = jnp.sum(summed[8:16], keepdims=True)
        if sweep == 0:
            ratio = jnp.zeros((1, 1), f32)
            step_size = norm_now / product
        else:
            ratio = norm_now / norm_before
            step_size = norm_now / (product - ratio * norm_now / step_size)
        norm_before = norm_now

        def update(c, carry, ratio=ratio, step_size=step_size, parity=parity, last=last):
            rows = chunk_rows(c)
            old = fields[0, rows]
            heading = old + ratio * direction[rows]
            solution_ref[rows, :] = solution_ref[rows, :] + step_size * heading
            if last:
                along = images[parity, 0, rows] + ratio * alongs[0, rows]
                residual_ref[rows, :] = old - step_size * along
                return carry
            direction[rows] = heading
            marks = None
            for which in range(3):
                along = images[parity, which, rows] + ratio * alongs[which, rows]
                value = fields[which, rows] - step_size * along
                alongs[which, rows] = along
                fields[which, rows] = value
                high, low = halves(value)
                field_high[which, rows] = high
                field_low[which, rows] = low
                if which == 0:
                    marks = fold(value * value)
            return carry + marks

        norm_marks = lax.fori_loop(0, CHUNKS, update, jnp.zeros((8, 128), f32))

    @pl.when(has_next)
    def _():
        for copy in hop_copies:
            copy.wait_send()


def body(left_ops, right_ops, hop_left, hop_right, v_left, v_right, zero_blocks, links, block_dims):
    width = left_ops.shape[-1]
    small = zero_blocks.shape[-1]
    nz = lax.axis_size("term")
    ns = lax.axis_size("sector")
    vmem = pl.BlockSpec(memory_space=pltpu.VMEM)
    smem = pl.BlockSpec(memory_space=pltpu.SMEM)
    dma = pltpu.SemaphoreType.DMA
    square = jax.ShapeDtypeStruct((width, width), f32)
    solution, residual = pl.pallas_call(
        functools.partial(kernel, nz, ns),
        out_shape=(square, square),
        in_specs=[smem, smem] + [vmem] * 7,
        out_specs=(vmem, vmem),
        scratch_shapes=[
            pltpu.VMEM((ns, small, small), bf16),
            pltpu.VMEM((width, width), f32),
            pltpu.VMEM((width, width), f32),
            pltpu.VMEM((3, 2, width, width), bf16),
            pltpu.VMEM((3, 2, width, width), bf16),
            pltpu.VMEM((3, width, width), bf16),
            pltpu.VMEM((3, width, width), bf16),
            pltpu.VMEM((3, width, width), f32),
            pltpu.VMEM((3, width, width), f32),
            pltpu.VMEM((width, width), f32),
            pltpu.VMEM((2, 3, width, width), f32),
            pltpu.VMEM((2, width, width), f32),
            pltpu.VMEM((2, width, width), f32),
            pltpu.VMEM((2, width, width), f32),
            pltpu.VMEM((ITERS, 16, 128), f32),
            pltpu.VMEM((ITERS, ns, 16, 128), f32),
            dma((ns,)),
            dma((ns,)),
            dma((2,)),
            dma((2,)),
            dma((2, CHUNKS)),
            dma((2, CHUNKS)),
            dma((2, CHUNKS)),
            dma((2, CHUNKS)),
            dma((2, 2, CHUNKS)),
            dma((2, 2, CHUNKS)),
            dma((ITERS, ns)),
            dma((ITERS, ns)),
        ],
        compiler_params=pltpu.CompilerParams(
            collective_id=0, has_side_effects=True, vmem_limit_bytes=56 * 1024 * 1024
        ),
        cost_estimate=pl.CostEstimate(
            flops=ITERS * 36 * width ** 3, bytes_accessed=24 * width * width, transcendentals=0
        ),
    )(
        links, block_dims, left_ops[0, 0], right_ops[0, 0], hop_left[0, 0], hop_right[0, 0],
        v_left[0, 0], v_right[0, 0], zero_blocks[0],
    )
    return solution[None], residual[None]


def solution(mesh):
    return jax.shard_map(
        body,
        mesh=mesh,
        in_specs=(
            P("term", "sector", None, None),
            P("term", "sector", None, None),
            P("term", "sector", None, None),
            P("term", "sector", None, None),
            P("term", "sector", None, None),
            P("term", "sector", None, None),
            P("sector", None, None),
            P("term", "sector"),
            P("sector"),
        ),
        out_specs=(P("sector", None, None), P("sector", None, None)),
        check_vma=False,
    )
```

time: 524 us -> 194 us (0.37); the launches traced: 518 us -> 194 us
  waiting for transfers between devices: 264 us -> 0 us
  Pallas kernels: 0 us -> 188 us
  blocking collectives: 128 us -> 0 us
  matrix products: 56.8 us -> 0 us
  starting transfers between devices: 26.4 us -> 0 us
  between operations: 25.7 us -> 1.94 us
  other arithmetic: 12 us -> 0 us
    pallas_call x0 -> x1, Pallas kernels: none -> 188 us  [body(): pl.pallas_call(functools.partial(kernel, nz, ns), out_shape=(square, squa...]
    reduce_scatter x4 -> x0, waiting for transfers between devices: 136 us -> none  [the longest x3 109 us: operate(): lax.psum_scatter(apply_terms(whole_rows, left_op, right_op, hop_in, hop_o...]
    all_gather x5 -> x0, waiting for transfers between devices: 128 us -> none  [the longest x3 70.9 us: operate(): whole_rows = lax.all_gather(vector, 'term', axis=0, tiled=True)]
    psum x3 -> x0, blocking collectives: 117 us -> none  [paired(): lax.psum((own_rows(vector * vector), own_rows(vector * image_vec)), ('ter...]
    dot_general x20 -> x0, matrix products: 56.8 us -> none  [the longest x3 10.5 us: apply_terms(): ahead = jnp.einsum('tij,jk->tik', hop_in, after, precision=exact)]
    ppermute x6 -> x0, starting transfers between devices: 13.8 us -> none  [shifted(): lax.ppermute(value, axis, [(source, source + steps) for source in range(f...]
    reduce_scatter x4 -> x0, starting transfers between devices: 12.4 us -> none  [the longest x3 12.4 us: operate(): lax.psum_scatter(apply_terms(whole_rows, left_op, right_op, hop_in, hop_o...]
    all_gather x1 -> x0, blocking collectives: 11.1 us -> none  [body(): everyone = lax.all_gather(zero_blocks, 'sector', axis=0, tiled=True)]
  transfers between devices with their start and end apart: 15 -> 0, of which waited for: 9 -> 0; matrix products, arithmetic and copies ran while one was open for 8% -> 0% of each run, Pallas kernels for 0% -> 0%
where the time goes in v1:
time: 194 us
  Pallas kernels  188 us (97%)
  local copies, waits for them, and re-layouts  3.32 us (2%)
  between operations  1.94 us (1%)
    pallas_call x1, Pallas kernels, body(): pl.pallas_call(functools.partial(kernel, nz, ns), out_shape=(square, squa...  188 us

profile of v1, /device:TPU:0, one launch (start us, length us, event | category | flops | bytes accessed | tf_op | source)
XLA Modules:
  0.0 193.5 jit_solution(211315578314946263)
XLA Ops:
  1.9 188.2 %shard_map.104 = (f32[512,512]{1,0:T(8,128)}, f32[512,512]{1,0:T(8,128)}) custom-call(s32[1,1]{1,0:T(1,128)S(6)} %copy.13.links_ref, s32[1]{0:T(128)S(6)} %copy.14.dims_ref, f32[512,512]{1,0:T(8,128)} %bitcast.11, f32[512,512]{1,0:T(8,128)} %bitcast.12, f32[512,512]{1,0:T(8,128)} %bitcast.13, f32[512,512]{1,0:T(8,128)} %bitcast.14, ...), custom_call_target="tpu_custom_call" | custom-call | flops 14495514624 | bytes 6291456 | tf_op jit(solution)/shard_map/pallas_call | solution.py:416
  190.2 0.0 copy-start
  190.2 2.4 %copy.15 = f32[1,512,512]{2,1,0:T(8,128)} copy(f32[1,512,512]{2,1,0:T(8,128)} %bitcast.10) | data formatting | bytes 2097152
  192.5 0.0 copy-done
  192.5 1.0 copy.16
Async XLA Ops:
  190.2 2.4 %copy-start = (f32[512,512]{1,0:T(8,128)S(1)}, f32[512,512]{1,0:T(8,128)}, u32[]{:S(2)}) copy-start(f32[512,512]{1,0:T(8,128)} %get-tuple-element.5) | copy-start | bytes 3145732

commit v2 on v1

--- a/solution.py
+++ b/solution.py
@@ -8,8 +8,10 @@
 from jax.sharding import PartitionSpec as P
 
 ITERS = 3
-CHUNKS = 8
+CHUNKS = 16
 GROUPS = 4
+LAG = 3
+LAG_STEP = 6
 
 level_gap = 2.5
 MESH = pl.DeviceIdType.MESH
@@ -169,8 +171,8 @@
         )
 
     def reduce_rows(parity, produce, finish, share):
-        most = 2 + 2 * (mid - 1)
-        lag = 2 + 2 * dist
+        most = LAG + LAG_STEP * (mid - 1)
+        lag = LAG + LAG_STEP * dist
 
         def one(c, carry):
             @pl.when(c < CHUNKS)

time: 194 us -> 184 us (0.948)
  Pallas kernels: 188 us -> 179 us
    pallas_call x1, Pallas kernels: 188 us -> 179 us  [body(): pl.pallas_call(functools.partial(kernel, nz, ns), out_shape=(square, squa...]
where the time goes in v2:
time: 184 us
  Pallas kernels  179 us (97%)
  local copies, waits for them, and re-layouts  3.32 us (2%)
  between operations  1.94 us (1%)
    pallas_call x1, Pallas kernels, body(): pl.pallas_call(functools.partial(kernel, nz, ns), out_shape=(square, squa...  179 us

profile of v2, /device:TPU:0, one launch (start us, length us, event | category | flops | bytes accessed | tf_op | source)
XLA Modules:
  0.0 184.2 jit_solution(13785098813407801362)
XLA Ops:
  1.9 178.9 %shard_map.104 = (f32[512,512]{1,0:T(8,128)}, f32[512,512]{1,0:T(8,128)}) custom-call(s32[1,1]{1,0:T(1,128)S(6)} %copy.13.links_ref, s32[1]{0:T(128)S(6)} %copy.14.dims_ref, f32[512,512]{1,0:T(8,128)} %bitcast.11, f32[512,512]{1,0:T(8,128)} %bitcast.12, f32[512,512]{1,0:T(8,128)} %bitcast.13, f32[512,512]{1,0:T(8,128)} %bitcast.14, ...), custom_call_target="tpu_custom_call" | custom-call | flops 14495514624 | bytes 6291456 | tf_op jit(solution)/shard_map/pallas_call | solution.py:418
  180.8 0.0 copy-start
  180.8 2.4 %copy.15 = f32[1,512,512]{2,1,0:T(8,128)} copy(f32[1,512,512]{2,1,0:T(8,128)} %bitcast.10) | data formatting | bytes 2097152
  183.2 0.0 copy-done
  183.2 1.0 copy.16
Async XLA Ops:
  180.8 2.4 %copy-start = (f32[512,512]{1,0:T(8,128)S(1)}, f32[512,512]{1,0:T(8,128)}, u32[]{:S(2)}) copy-start(f32[512,512]{1,0:T(8,128)} %get-tuple-element.5) | copy-start | bytes 3145732
